TPU v7x, 256 devices: a whole 4x4x8 slice. The times are simulated.
256 devices in a mesh: adapter: 32 (over z, x), feature: 8 (over y, core).
Axes of the slice: x: 4, y: 4, z: 8, core: 2. Of those that a mesh axis runs over, the one named last changes fastest.
Arguments:
- adapter_down: bfloat16 [512, 16, 8192], P('adapter', None, 'feature'), may hold values from -6 to 6
- adapter_up: bfloat16 [512, 16, 8192], P('adapter', None, 'feature'), may hold values from -6 to 6
- fisher: float32 [512], P('adapter'), may hold values from 0.1 to 10
- init_v: float32 [8192, 64], P('feature'), may hold values from -0.0625 to 0.0625
- init_u: float32 [8192, 64], P('feature'), may hold values from -0.0625 to 0.0625
- prompt_rows: bfloat16 [16384, 8192], P('adapter', 'feature'), may hold values from -6 to 6
- request_ids: int32 [128], P('adapter'), may hold values from 0 to 511
Outputs:
- served: bfloat16 [16384, 8192], P('adapter', 'feature')
All inputs are finite; a program needn't handle non-finite values.
Results may differ from a plain program's by a relative error of at most 0.025.
Values may be sent and summed in bfloat16 or wider, within the bound.
No kernel may reach another device: no remote copies, remote signals or barrier semaphores. Data moves between devices by JAX's collectives and lax.ppermute only.
A program may use at most 64 MiB of HBM per device.

v0:
```python
import jax
import jax.numpy as jnp
from jax import lax
from jax.sharding import PartitionSpec as P

SWEEPS = 3


highest = lax.Precision.HIGHEST


def in_blocks(shard, dim, count):
    dims = shard.shape
    parts = shard.reshape(*dims[:dim], count, dims[dim] // count, *dims[dim + 1 :])
    return jnp.moveaxis(parts, dim, 0)


def sum_at_owner(shard, axis, dim):
    count = lax.axis_size(axis)
    parts = lax.all_to_all(in_blocks(shard, dim, count), axis, 0, 0, tiled=True)
    return jnp.sum(parts, axis=0)


def filled_up(lines, count):
    spare = -lines.shape[0] % count
    if not spare:
        return lines
    return jnp.concatenate([lines, jnp.zeros((spare, *lines.shape[1:]), lines.dtype)])


def copy_for_each(shard, axis):
    count = lax.axis_size(axis)
    return lax.all_to_all(
        jnp.broadcast_to(shard[None], (count, *shard.shape)), axis, 0, 0, tiled=True
    )


def in_order(parts, dim):
    dims = list(parts.shape[1:])
    dims[dim] *= parts.shape[0]
    return jnp.moveaxis(parts, 0, dim).reshape(dims)


def gather_directly(shard, axis, dim):
    parts = copy_for_each(shard, axis)
    return in_order(parts, dim)


def sum_by_parts(shard, axes):
    lines = shard.reshape(-1, shard.shape[-1])
    own = sum_at_owner(filled_up(lines, lax.axis_size(axes)), axes, 0)
    whole = gather_directly(own, axes, 0)
    return whole[: len(lines)].reshape(shard.shape)


def taken_together(shard, axis):
    everything = copy_for_each(shard, axis)
    return jnp.sum(everything, axis=0)


def sent_and_summed(shard, axis, dim):
    count = lax.axis_size(axis)
    parts = lax.all_to_all(in_blocks(shard, dim, count), axis, 0, 0, tiled=True)
    return jnp.sum(parts.astype(jnp.float32), axis=0)


def project(adapter_stack, basis_low):
    flat = adapter_stack.reshape(-1, adapter_stack.shape[-1])
    result = jnp.dot(flat, basis_low, preferred_element_type=jnp.float32)
    return result.reshape(adapter_stack.shape[0], adapter_stack.shape[1], -1)


def core_of(cols_q, rows_p):
    return jnp.einsum("irk,irl->ikl", cols_q, rows_p, precision=highest)


def numerator(adapter_stack, weighted):
    flat = adapter_stack.reshape(-1, adapter_stack.shape[-1])
    terms = weighted.reshape(-1, weighted.shape[-1])
    return lax.dot_general(
        flat, terms, (((0,), (0,)), ((), ())), preferred_element_type=jnp.float32
    )


def solve_with(gram_sum, matrix):
    factor = jnp.linalg.cholesky(gram_sum)
    return lax.linalg.triangular_solve(
        factor, matrix, left_side=False, lower=True, transpose_a=True
    )


def renew(local_term):
    full_term = sum_by_parts(local_term, "adapter")
    gram_sum = taken_together(jnp.dot(full_term.T, full_term, precision=highest), "feature")
    return solve_with(gram_sum, full_term)


def down_sum(adapter_down, basis_v):
    return taken_together(project(adapter_down, basis_v.astype(jnp.bfloat16)), "feature")


def up_sum(adapter_up, basis_u):
    return taken_together(project(adapter_up, basis_u.astype(jnp.bfloat16)), "feature")


def on_device(adapter_down, adapter_up, fisher, init_v, init_u, prompt_rows, request_ids):
    basis_v = init_v
    basis_u = init_u
    weights = fisher[:, None, None]
    cols_q = up_sum(adapter_up, basis_u)
    for sweep_index in range(SWEEPS):
        rows_p = down_sum(adapter_down, basis_v)
        core_stack = core_of(cols_q, rows_p)
        weighted = (
            weights * jnp.einsum("irl,ikl->irk", rows_p, core_stack, precision=highest)
        ).astype(jnp.bfloat16)
        basis_u = renew(numerator(adapter_up, weighted))
        cols_q = up_sum(adapter_up, basis_u)
        core_stack = core_of(cols_q, rows_p)
        weighted = (
            weights * jnp.einsum("irk,ikl->irl", cols_q, core_stack, precision=highest)
        ).astype(jnp.bfloat16)
        basis_v = renew(numerator(adapter_down, weighted))
    rows_p = down_sum(adapter_down, basis_v)
    final_cores = core_of(cols_q, rows_p).astype(jnp.bfloat16)
    count_local = final_cores.shape[0]
    basis_width = final_cores.shape[1]
    flat_cores = final_cores.reshape(count_local, basis_width * basis_width)
    offset = lax.axis_index("adapter") * count_local
    local_range = offset + jnp.arange(count_local, dtype=jnp.int32)
    every_id = gather_directly(request_ids, "adapter", 0)
    onehot = (every_id[:, None] == local_range[None, :]).astype(jnp.bfloat16)
    slice_width = flat_cores.shape[1] // lax.axis_size("feature")
    core_part = lax.dynamic_slice_in_dim(
        flat_cores, lax.axis_index("feature") * slice_width, slice_width, 1
    )
    picked = jnp.dot(onehot, core_part, preferred_element_type=jnp.float32)
    own_part = sent_and_summed(picked.astype(jnp.bfloat16), "adapter", 0).astype(jnp.bfloat16)
    own_cores = gather_directly(own_part, "feature", 1)
    partial_rows = jnp.dot(
        prompt_rows, basis_v.astype(jnp.bfloat16), preferred_element_type=jnp.float32
    )
    hidden = taken_together(partial_rows, "feature").astype(jnp.bfloat16)
    blocks = own_cores.shape[0]
    blocked = hidden.reshape(blocks, -1, basis_width)
    mixed_rows = jnp.einsum(
        "bnl,bkl->bnk",
        blocked,
        own_cores.reshape(blocks, basis_width, basis_width),
        preferred_element_type=jnp.float32,
    ).astype(jnp.bfloat16)
    served = jnp.dot(
        mixed_rows.reshape(-1, basis_width),
        basis_u.astype(jnp.bfloat16).T,
        preferred_element_type=jnp.float32,
    )
    return served.astype(jnp.bfloat16)


def solution(mesh):
    placed = (
        P("adapter", None, "feature"),
        P("adapter", None, "feature"),
        P("adapter"),
        P("feature", None),
        P("feature", None),
        P("adapter", "feature"),
        P("adapter"),
    )
    return jax.shard_map(
        on_device, mesh=mesh, in_specs=placed, out_specs=P("adapter", "feature"), check_vma=False
    )
```

profile of v0, /device:TPU:1, one launch (start us, length us, event | category | flops | bytes accessed | tf_op | source)
XLA Modules:
  0.0 591.7 jit_solution(17096553244458397349)
XLA Ops:
  3.0 6.6 %all-to-all-start.1 = ((f32[8,1,16384]{2,1,0:T(1,128)}), f32[8,1,16384]{2,1,0:T(1,128)S(1)}, u32[]{:S(2)}, u32[]{:S(2)}) async-start(f32[8,1,16384]{2,1,0:T(1,128)} %reshape.192), calls=%async_computation.1 | async-start | bytes 1048576 | tf_op jit(solution)/shard_map/all_to_all | solution.py:33
  11.5 7.7 %all-to-all-done.1 = f32[8,1,16384]{2,1,0:T(1,128)S(1)} async-done(((f32[8,1,16384]{2,1,0:T(1,128)}), f32[8,1,16384]{2,1,0:T(1,128)S(1)}, u32[]{:S(2)}, u32[]{:S(2)}) %all-to-all-start.1) | async-done | bytes 524320 | tf_op jit(solution)/shard_map/all_to_all | solution.py:33
  19.2 4.9 all-to-all-start
  28.1 5.6 all-to-all-done
  33.7 3.0 reduce.9
  42.2 21.2 %all_to_all.151 = f32[32,1,2048]{2,1,0:T(1,128)S(1)} all-to-all(f32[32,1,2048]{2,1,0:T(1,128)S(1)} %reshape.194), channel_id=1, replica_groups=mesh['adapter'=32,'feature'=8] {'adapter'}, dimensions={0} | all-to-all | bytes 524288 | tf_op jit(solution)/shard_map/all_to_all | solution.py:20
  65.4 15.0 %all_to_all.152 = f32[32,1,2048]{2,1,0:T(1,128)S(1)} all-to-all(f32[32,1,2048]{2,1,0:T(1,128)S(1)} %reshape.196), channel_id=1, replica_groups=mesh['adapter'=32,'feature'=8] {'adapter'}, dimensions={0} | all-to-all | bytes 524288 | tf_op jit(solution)/shard_map/all_to_all | solution.py:33
  83.2 11.6 %all_to_all.153 = f32[8,1,4096]{2,1,0:T(1,128)S(1)} all-to-all(f32[8,1,4096]{2,1,0:T(1,128)S(1)} %reshape.198), channel_id=1, replica_groups=mesh['adapter'=32,'feature'=8] {'feature'}, dimensions={0} | all-to-all | bytes 262144 | tf_op jit(solution)/shard_map/all_to_all | solution.py:33
  96.0 5.8 cholesky.104
  103.2 4.9 custom-call.10
  110.8 13.6 %all_to_all.154 = f32[8,1,16384]{2,1,0:T(1,128)S(1)} all-to-all(f32[8,1,16384]{2,1,0:T(1,128)} %reshape.200), channel_id=1, replica_groups=mesh['adapter'=32,'feature'=8] {'feature'}, dimensions={0} | all-to-all | bytes 1048576 | tf_op jit(solution)/shard_map/all_to_all | solution.py:33
  131.2 13.6 %all_to_all.155 = f32[32,1,2048]{2,1,0:T(1,128)S(1)} all-to-all(f32[32,1,2048]{2,1,0:T(1,128)S(1)} %reshape.202), channel_id=1, replica_groups=mesh['adapter'=32,'feature'=8] {'adapter'}, dimensions={0} | all-to-all | bytes 524288 | tf_op jit(solution)/shard_map/all_to_all | solution.py:20
  146.7 15.6 %all_to_all.156 = f32[32,1,2048]{2,1,0:T(1,128)S(1)} all-to-all(f32[32,1,2048]{2,1,0:T(1,128)S(1)} %reshape.204), channel_id=1, replica_groups=mesh['adapter'=32,'feature'=8] {'adapter'}, dimensions={0} | all-to-all | bytes 524288 | tf_op jit(solution)/shard_map/all_to_all | solution.py:33
  165.0 11.6 %all_to_all.157 = f32[8,1,4096]{2,1,0:T(1,128)S(1)} all-to-all(f32[8,1,4096]{2,1,0:T(1,128)S(1)} %reshape.206), channel_id=1, replica_groups=mesh['adapter'=32,'feature'=8] {'feature'}, dimensions={0} | all-to-all | bytes 262144 | tf_op jit(solution)/shard_map/all_to_all | solution.py:33
  177.9 5.8 cholesky.115
  185.1 4.9 custom-call.11
  192.6 13.6 %all_to_all.158 = f32[8,1,16384]{2,1,0:T(1,128)S(1)} all-to-all(f32[8,1,16384]{2,1,0:T(1,128)} %reshape.208), channel_id=1, replica_groups=mesh['adapter'=32,'feature'=8] {'feature'}, dimensions={0} | all-to-all | bytes 1048576 | tf_op jit(solution)/shard_map/all_to_all | solution.py:33
  213.4 13.5 %all_to_all.159 = f32[32,1,2048]{2,1,0:T(1,128)S(1)} all-to-all(f32[32,1,2048]{2,1,0:T(1,128)S(1)} %reshape.210), channel_id=1, replica_groups=mesh['adapter'=32,'feature'=8] {'adapter'}, dimensions={0} | all-to-all | bytes 524288 | tf_op jit(solution)/shard_map/all_to_all | solution.py:20
  228.9 15.6 %all_to_all.160 = f32[32,1,2048]{2,1,0:T(1,128)S(1)} all-to-all(f32[32,1,2048]{2,1,0:T(1,128)S(1)} %reshape.212), channel_id=1, replica_groups=mesh['adapter'=32,'feature'=8] {'adapter'}, dimensions={0} | all-to-all | bytes 524288 | tf_op jit(solution)/shard_map/all_to_all | solution.py:33
  247.2 11.8 %all_to_all.161 = f32[8,1,4096]{2,1,0:T(1,128)S(1)} all-to-all(f32[8,1,4096]{2,1,0:T(1,128)S(1)} %reshape.214), channel_id=1, replica_groups=mesh['adapter'=32,'feature'=8] {'feature'}, dimensions={0} | all-to-all | bytes 262144 | tf_op jit(solution)/shard_map/all_to_all | solution.py:33
  260.3 5.8 cholesky.126
  267.5 4.9 custom-call.12
  275.0 13.6 %all_to_all.162 = f32[8,1,16384]{2,1,0:T(1,128)S(1)} all-to-all(f32[8,1,16384]{2,1,0:T(1,128)} %reshape.216), channel_id=1, replica_groups=mesh['adapter'=32,'feature'=8] {'feature'}, dimensions={0} | all-to-all | bytes 1048576 | tf_op jit(solution)/shard_map/all_to_all | solution.py:33
  295.4 13.6 %all_to_all.163 = f32[32,1,2048]{2,1,0:T(1,128)S(1)} all-to-all(f32[32,1,2048]{2,1,0:T(1,128)S(1)} %reshape.218), channel_id=1, replica_groups=mesh['adapter'=32,'feature'=8] {'adapter'}, dimensions={0} | all-to-all | bytes 524288 | tf_op jit(solution)/shard_map/all_to_all | solution.py:20
  311.0 15.6 %all_to_all.164 = f32[32,1,2048]{2,1,0:T(1,128)S(1)} all-to-all(f32[32,1,2048]{2,1,0:T(1,128)S(1)} %reshape.220), channel_id=1, replica_groups=mesh['adapter'=32,'feature'=8] {'adapter'}, dimensions={0} | all-to-all | bytes 524288 | tf_op jit(solution)/shard_map/all_to_all | solution.py:33
  329.3 11.6 %all_to_all.165 = f32[8,1,4096]{2,1,0:T(1,128)S(1)} all-to-all(f32[8,1,4096]{2,1,0:T(1,128)S(1)} %reshape.222), channel_id=1, replica_groups=mesh['adapter'=32,'feature'=8] {'feature'}, dimensions={0} | all-to-all | bytes 262144 | tf_op jit(solution)/shard_map/all_to_all | solution.py:33
  342.1 5.8 cholesky.137
  349.3 4.9 custom-call.13
  356.9 13.6 %all_to_all.166 = f32[8,1,16384]{2,1,0:T(1,128)S(1)} all-to-all(f32[8,1,16384]{2,1,0:T(1,128)} %reshape.224), channel_id=1, replica_groups=mesh['adapter'=32,'feature'=8] {'feature'}, dimensions={0} | all-to-all | bytes 1048576 | tf_op jit(solution)/shard_map/all_to_all | solution.py:33
  377.6 13.5 %all_to_all.167 = f32[32,1,2048]{2,1,0:T(1,128)S(1)} all-to-all(f32[32,1,2048]{2,1,0:T(1,128)S(1)} %reshape.226), channel_id=1, replica_groups=mesh['adapter'=32,'feature'=8] {'adapter'}, dimensions={0} | all-to-all | bytes 524288 | tf_op jit(solution)/shard_map/all_to_all | solution.py:20
  393.1 15.6 %all_to_all.168 = f32[32,1,2048]{2,1,0:T(1,128)S(1)} all-to-all(f32[32,1,2048]{2,1,0:T(1,128)S(1)} %reshape.228), channel_id=1, replica_groups=mesh['adapter'=32,'feature'=8] {'adapter'}, dimensions={0} | all-to-all | bytes 524288 | tf_op jit(solution)/shard_map/all_to_all | solution.py:33
  411.5 11.6 %all_to_all.169 = f32[8,1,4096]{2,1,0:T(1,128)S(1)} all-to-all(f32[8,1,4096]{2,1,0:T(1,128)S(1)} %reshape.230), channel_id=1, replica_groups=mesh['adapter'=32,'feature'=8] {'feature'}, dimensions={0} | all-to-all | bytes 262144 | tf_op jit(solution)/shard_map/all_to_all | solution.py:33
  424.3 5.8 cholesky.148
  431.5 4.9 custom-call.14
  438.3 12.6 %all_to_all.170 = f32[8,1,16384]{2,1,0:T(1,128)S(1)} all-to-all(f32[8,1,16384]{2,1,0:T(1,128)S(1)} %reshape.232), channel_id=1, replica_groups=mesh['adapter'=32,'feature'=8] {'feature'}, dimensions={0} | all-to-all | bytes 1048576 | tf_op jit(solution)/shard_map/all_to_all | solution.py:33
  455.7 13.5 %all_to_all.171 = f32[32,1,2048]{2,1,0:T(1,128)S(1)} all-to-all(f32[32,1,2048]{2,1,0:T(1,128)S(1)} %reshape.234), channel_id=1, replica_groups=mesh['adapter'=32,'feature'=8] {'adapter'}, dimensions={0} | all-to-all | bytes 524288 | tf_op jit(solution)/shard_map/all_to_all | solution.py:20
  471.2 15.6 %all_to_all.172 = f32[32,1,2048]{2,1,0:T(1,128)S(1)} all-to-all(f32[32,1,2048]{2,1,0:T(1,128)S(1)} %reshape.236), channel_id=1, replica_groups=mesh['adapter'=32,'feature'=8] {'adapter'}, dimensions={0} | all-to-all | bytes 524288 | tf_op jit(solution)/shard_map/all_to_all | solution.py:33
  489.6 11.4 %all_to_all.173 = f32[8,1,4096]{2,1,0:T(1,128)S(1)} all-to-all(f32[8,1,4096]{2,1,0:T(1,128)S(1)} %reshape.238), channel_id=1, replica_groups=mesh['adapter'=32,'feature'=8] {'feature'}, dimensions={0} | all-to-all | bytes 262144 | tf_op jit(solution)/shard_map/all_to_all | solution.py:33
  501.6 4.1 all-to-all-start.26
  507.0 5.8 cholesky.159
  514.1 4.9 custom-call.15
  521.7 4.3 all-to-all-start.27
  527.4 8.1 %all-to-all-done.27 = f32[8,1,16384]{2,1,0:T(1,128)S(1)} async-done(((f32[8,1,16384]{2,1,0:T(1,128)}), f32[8,1,16384]{2,1,0:T(1,128)S(1)}, u32[]{:S(2)}, u32[]{:S(2)}) %all-to-all-start.27) | async-done | bytes 524320 | tf_op jit(solution)/shard_map/all_to_all | solution.py:33
  539.5 18.6 %all_to_all.174 = bf16[32,4,512]{2,1,0:T(4,128)(2,1)S(1)} all-to-all(bf16[32,4,512]{2,1,0:T(4,128)(2,1)S(1)} %reshape.143), channel_id=1, replica_groups=mesh['adapter'=32,'feature'=8] {'adapter'}, dimensions={0} | all-to-all | bytes 262144 | tf_op jit(solution)/shard_map/all_to_all | solution.py:63
  558.8 5.6 all-to-all-start.29
  564.9 4.3 all-to-all-done.29
  570.3 4.2 all-to-all-start.25
  574.6 15.0 %all-to-all-done.25 = f32[8,512,64]{1,2,0:T(8,128)S(1)} async-done(((f32[8,512,64]{1,2,0:T(8,128)}), f32[8,512,64]{1,2,0:T(8,128)S(1)}, u32[]{:S(2)}, u32[]{:S(2)}) %all-to-all-start.25) | async-done | bytes 1048608 | tf_op jit(solution)/shard_map/all_to_all | solution.py:33
  (231 shorter events, 115.0 us)
Async XLA Ops:
  0.0 564.4 %copy-start = (bf16[512,1024]{1,0:T(8,128)(2,1)S(1)}, bf16[512,1024]{1,0:T(8,128)(2,1)}, u32[]{:S(2)}) copy-start(bf16[512,1024]{1,0:T(8,128)(2,1)} %param.15) | copy-start | bytes 3145732
  1.6 8.1 %copy-start.2 = (bf16[16,16,1024]{2,1,0:T(8,128)(2,1)S(1)}, bf16[16,16,1024]{2,1,0:T(8,128)(2,1)}, u32[]{:S(2)}) copy-start(bf16[16,16,1024]{2,1,0:T(8,128)(2,1)} %param.10) | copy-start | bytes 1572868
  1.6 8.1 %copy-start.4 = (f32[1024,64]{0,1:T(8,128)S(1)}, f32[1024,64]{0,1:T(8,128)}, u32[]{:S(2)}) copy-start(f32[1024,64]{0,1:T(8,128)} %param.13) | copy-start | bytes 786436
  3.0 16.1 %all-to-all-start.1 = ((f32[8,1,16384]{2,1,0:T(1,128)}), f32[8,1,16384]{2,1,0:T(1,128)S(1)}, u32[]{:S(2)}, u32[]{:S(2)}) async-start(f32[8,1,16384]{2,1,0:T(1,128)} %reshape.192), calls=%async_computation.1 | async-start | bytes 1048576 | tf_op jit(solution)/shard_map/all_to_all | solution.py:33
  19.2 4.9 copy-start.3
  19.2 14.5 %all-to-all-start = ((f32[8,1,16384]{2,1,0:T(1,128)}), f32[8,1,16384]{2,1,0:T(1,128)}, u32[]{:S(2)}, u32[]{:S(2)}) async-start(f32[8,1,16384]{2,1,0:T(1,128)} %reshape.190), calls=%async_computation | async-start | bytes 1048576 | tf_op jit(solution)/shard_map/all_to_all | solution.py:33
  38.1 2.4 copy-start.5
  39.5 2.0 copy-start.1
  488.3 12.7 %copy-start.6 = (s32[4]{0:T(128)S(1)}, s32[4]{0:T(128)}, u32[]{:S(2)}) copy-start(s32[4]{0:T(128)} %param.16) | copy-start | bytes 52
  501.6 20.1 %all-to-all-start.26 = ((s32[32,1,4]{2,1,0:T(1,128)}), s32[32,1,4]{2,1,0:T(1,128)S(1)}, u32[]{:S(2)}, u32[]{:S(2)}) async-start(s32[32,1,4]{2,1,0:T(1,128)} %broadcast_in_dim.84), calls=%async_computation.26 | async-start | bytes 32768 | tf_op jit(solution)/shard_map/all_to_all | solution.py:33
  521.7 13.8 %all-to-all-start.27 = ((f32[8,1,16384]{2,1,0:T(1,128)}), f32[8,1,16384]{2,1,0:T(1,128)S(1)}, u32[]{:S(2)}, u32[]{:S(2)}) async-start(f32[8,1,16384]{2,1,0:T(1,128)} %reshape.240), calls=%async_computation.27 | async-start | bytes 1048576 | tf_op jit(solution)/shard_map/all_to_all | solution.py:33
  558.8 10.3 %all-to-all-start.29 = ((bf16[8,4,512]{2,1,0:T(4,128)(2,1)}), bf16[8,4,512]{2,1,0:T(4,128)(2,1)S(1)}, u32[]{:S(2)}, u32[]{:S(2)}) async-start(bf16[8,4,512]{2,1,0:T(4,128)(2,1)} %broadcast_in_dim.87), calls=%async_computation.29 | async-start | bytes 65536 | tf_op jit(solution)/shard_map/all_to_all | solution.py:33
  570.3 19.3 %all-to-all-start.25 = ((f32[8,512,64]{1,2,0:T(8,128)}), f32[8,512,64]{1,2,0:T(8,128)S(1)}, u32[]{:S(2)}, u32[]{:S(2)}) async-start(f32[8,512,64]{1,2,0:T(8,128)} %broadcast_in_dim.83), calls=%async_computation.25 | async-start | bytes 2097152 | tf_op jit(solution)/shard_map/all_to_all | solution.py:33
where the time goes:
time: 602 us; the launch traced here: 592 us
  blocking collectives  337 us (56%)
  other arithmetic  119 us (20%)
  waiting for transfers between devices  40.6 us (7%)
  local copies, waits for them, and re-layouts  34.7 us (6%)
  starting transfers between devices  29.7 us (5%)
  matrix products  29.1 us (5%)
    all_to_all x17, blocking collectives, copy_for_each(): lax.all_to_all(jnp.broadcast_to(shard[None], (count, *shard.shape)), axis...  230 us
    all_to_all x6, blocking collectives, sum_at_owner(): parts = lax.all_to_all(in_blocks(shard, dim, count), axis, 0, 0, tiled=True)  89 us
    all_to_all x6, waiting for transfers between devices, copy_for_each(): lax.all_to_all(jnp.broadcast_to(shard[None], (count, *shard.shape)), axis...  40.6 us
    another operation x18, other arithmetic, solve_with(): factor = jnp.linalg.cholesky(gram_sum)  39.1 us
    all_to_all x21, other arithmetic, copy_for_each(): lax.all_to_all(jnp.broadcast_to(shard[None], (count, *shard.shape)), axis...  35.8 us
    another operation x12, other arithmetic, solve_with(): lax.linalg.triangular_solve(factor, matrix, left_side=False, lower=True,...  33.3 us
    all_to_all x6, starting transfers between devices, copy_for_each(): lax.all_to_all(jnp.broadcast_to(shard[None], (count, *shard.shape)), axis...  29.7 us
    unnamed x66, local copies, waits for them, and re-layouts  27.4 us
  transfers between devices with their start and end apart: 6, of which 5 were waited for; matrix products, arithmetic and copies ran while one was open for 4% of the time, Pallas kernels for 0%

commit v1 on v0

v1 whole, which is shorter than its diff:
```python
import jax
import jax.numpy as jnp
from jax import lax
from jax.experimental import pallas as pl
from jax.experimental.pallas import tpu as pltpu
from jax.sharding import PartitionSpec as P

SWEEPS = 3
RANK = 16
BF = jnp.bfloat16
F32 = jnp.float32
highest = lax.Precision.HIGHEST


def call(body, outs, *args):
    whole = pl.BlockSpec(memory_space=pltpu.VMEM)
    single = not isinstance(outs, (list, tuple))
    return pl.pallas_call(
        body,
        out_shape=outs,
        in_specs=[whole] * len(args),
        out_specs=whole if single else [whole] * len(outs),
        compiler_params=pltpu.CompilerParams(vmem_limit_bytes=40 * 1024 * 1024),
    )(*args)


def shape(dims, dtype):
    return jax.ShapeDtypeStruct(dims, dtype)


def dot_nt(a, b, precision=None):
    return lax.dot_general(
        a, b, (((1,), (1,)), ((), ())), preferred_element_type=F32, precision=precision
    )


def dot_tn(a, b, precision=None):
    return lax.dot_general(
        a, b, (((0,), (0,)), ((), ())), preferred_element_type=F32, precision=precision
    )


def dot_nn(a, b, precision=None):
    return jnp.dot(a, b, preferred_element_type=F32, precision=precision)


def inverse_factor(gram):
    size = gram.shape[0]
    rows = lax.broadcasted_iota(jnp.int32, (size, size), 0)
    lanes = lax.broadcasted_iota(jnp.int32, (size, size), 1)
    work = jnp.concatenate([gram, (rows == lanes).astype(F32)], axis=1)
    row_of = lax.broadcasted_iota(jnp.int32, work.shape, 0)
    for k in range(size - 1):
        row = work[k : k + 1, :]
        scaled = row / work[k : k + 1, k : k + 1]
        column = jnp.where(row_of > k, jnp.broadcast_to(work[:, k : k + 1], work.shape), 0.0)
        work = work - column * scaled
    diagonal = jnp.sum(jnp.where(rows == lanes, work[:, :size], 0.0), axis=1, keepdims=True)
    return work[:, size:] * lax.rsqrt(diagonal)


def write_copies(ref, value):
    for i in range(ref.shape[0]):
        ref[i] = value


def summed(ref):
    total = ref[0].astype(F32)
    for i in range(1, ref.shape[0]):
        total = total + ref[i].astype(F32)
    return total


def write_tiles(ref, value):
    across = value.shape[1] // 128
    for i in range(ref.shape[0]):
        r, c = divmod(i, across)
        ref[i] = value[16 * r : 16 * r + 16, 128 * c : 128 * c + 128].astype(BF)


def read_tiles(ref, width):
    across = width // 128
    down = ref.shape[0] // across
    return jnp.concatenate(
        [
            jnp.concatenate([ref[r * across + c] for c in range(across)], axis=1)
            for r in range(down)
        ],
        axis=0,
    )


def halves(gram):
    high = gram.astype(BF)
    low = (gram - high.astype(F32)).astype(BF)
    return jnp.concatenate([high, low], axis=1)


def weighted_terms(fresh, other, fisher_row):
    count = fresh.shape[1]
    inner = dot_tn(fresh, fresh, highest)
    a = lax.broadcasted_iota(jnp.int32, (count, count), 0) // RANK
    b = lax.broadcasted_iota(jnp.int32, (count, count), 1) // RANK
    inner = jnp.where(a == b, inner, 0.0)
    return (dot_nn(other, inner, highest) * fisher_row).astype(BF)


def start_body(down, up, vt, ut, out):
    q = dot_nt(ut[...], up[...]).astype(BF)
    p = dot_nt(vt[...], down[...]).astype(BF)
    write_copies(out, jnp.concatenate([q, p], axis=1))


def first_body(parts, stack, fisher_row, tiles, q_out, p_out):
    total = summed(parts)
    count = total.shape[1] // 2
    q, p = total[:, :count], total[:, count:]
    q_out[...] = q
    p_out[...] = p
    terms = weighted_terms(p, q, fisher_row[...])
    write_tiles(tiles, dot_nn(terms, stack[...]))


def sum_body(parts, out):
    write_copies(out, summed(parts).astype(BF))


def project_body(tiles, stack, out):
    numer = read_tiles(tiles, stack.shape[1])
    y = dot_nt(numer, stack[...]).astype(BF)
    gram = dot_nt(numer, numer)
    write_copies(out, jnp.concatenate([y, halves(gram)], axis=1))


def split_gram(total, at, size):
    return total[:, at : at + size] + total[:, at + size : at + 2 * size]


def renew_body(parts, other, stack, fisher_row, tiles, fresh_out):
    total = summed(parts)
    size, count = other.shape
    inverse = inverse_factor(split_gram(total, count, size))
    fresh = dot_nn(inverse, total[:, :count], highest)
    fresh_out[...] = fresh
    terms = weighted_terms(fresh, other[...], fisher_row[...])
    write_tiles(tiles, dot_nn(terms, stack[...]))


def last_renew_body(parts, other, stack, fisher_row, numer_tiles, tiles, fresh_out, basis_out):
    total = summed(parts)
    size, count = other.shape
    inverse = inverse_factor(split_gram(total, count, size))
    fresh = dot_nn(inverse, total[:, :count], highest)
    fresh_out[...] = fresh
    terms = weighted_terms(fresh, other[...], fisher_row[...])
    write_tiles(tiles, dot_nn(terms, stack[...]))
    numer = read_tiles(numer_tiles, stack.shape[1]).astype(F32)
    basis_out[...] = dot_nn(inverse, numer, highest).astype(BF)


def pick_body(tiles, stack, prompts, q_ref, ids, picked, rest):
    numer = read_tiles(tiles, stack.shape[1])
    z = dot_nt(stack[...], numer).astype(BF)
    q = q_ref[...].T.astype(BF)
    both = jnp.concatenate([z, q], axis=1)
    count = both.shape[0]
    wanted = picked.shape[0] * picked.shape[1]
    r = lax.broadcasted_iota(jnp.int32, (wanted, count), 0)
    c = lax.broadcasted_iota(jnp.int32, (wanted, count), 1)
    hot = ids[...] * RANK + (r & (RANK - 1)) == c
    chosen = dot_nn(hot.astype(F32).astype(BF), both).astype(BF)
    each = picked.shape[1]
    for i in range(picked.shape[0]):
        picked[i] = chosen[i * each : (i + 1) * each]
    hidden = dot_nt(numer, prompts[...]).astype(BF)
    rest[...] = jnp.concatenate([hidden, halves(dot_nt(numer, numer))], axis=1)


def join_body(parts, rest, out, own):
    total = summed(parts).astype(BF)
    own[...] = total
    write_copies(out, jnp.concatenate([rest[...], total], axis=1))


def serve_body(parts, own, basis, out):
    total = summed(parts)
    size = total.shape[0]
    rows = out.shape[0]
    inverse = inverse_factor(split_gram(total, rows, size))
    hidden = dot_nn(inverse, total[:, :rows], highest).astype(BF)
    z = total[:, rows + 2 * size : rows + 3 * size]
    p = dot_nt(z, inverse, highest)
    q = own[...][:, size:].astype(F32)
    blocks = own.shape[0] // RANK
    each = rows // blocks
    for j in range(blocks):
        take = slice(j * RANK, (j + 1) * RANK)
        core = dot_tn(q[take], p[take], highest).astype(BF)
        mixed = dot_nn(core, hidden[:, j * each : (j + 1) * each]).astype(BF)
        out[j * each : (j + 1) * each, :] = dot_tn(mixed, basis[...]).astype(BF)


def swap(parts, axis):
    return lax.all_to_all(parts, axis, 0, 0, tiled=True)


def on_device(adapter_down, adapter_up, fisher, init_v, init_u, prompt_rows, request_ids):
    ways = lax.axis_size("adapter")
    shares = lax.axis_size("feature")
    width = adapter_down.shape[-1]
    size = init_v.shape[1]
    down = adapter_down.reshape(-1, width)
    up = adapter_up.reshape(-1, width)
    count = down.shape[0]
    rows = prompt_rows.shape[0]
    fisher_row = jnp.repeat(fisher, RANK)[None, :]
    tile_shape = shape((ways, size * width // ways // 128, 128), BF)
    flat = shape((size, count), F32)

    every_id = lax.all_to_all(
        jnp.broadcast_to(request_ids[None], (ways, *request_ids.shape)), "adapter", 0, 0, tiled=True
    ).reshape(-1)
    local_id = every_id - lax.axis_index("adapter") * fisher.shape[0]
    pick_rows = jnp.repeat(local_id, RANK)[:, None]

    def reduced(tiles):
        parts = swap(tiles, "adapter")
        return swap(call(sum_body, tile_shape, parts), "adapter")

    def projected(numer, stack):
        parts = call(project_body, shape((shares, size, count + 2 * size), BF), numer, stack)
        return swap(parts, "feature")

    parts = call(
        start_body,
        shape((shares, size, 2 * count), BF),
        down,
        up,
        init_v.T.astype(BF),
        init_u.T.astype(BF),
    )
    tiles, q, p = call(
        first_body, [tile_shape, flat, flat], swap(parts, "feature"), up, fisher_row
    )
    for sweep in range(SWEEPS):
        numer = reduced(tiles)
        parts = projected(numer, up)
        if sweep < SWEEPS - 1:
            tiles, q = call(renew_body, [tile_shape, flat], parts, p, down, fisher_row)
            parts = projected(reduced(tiles), down)
            tiles, p = call(renew_body, [tile_shape, flat], parts, q, up, fisher_row)
        else:
            tiles, q, basis = call(
                last_renew_body,
                [tile_shape, flat, shape((size, width), BF)],
                parts,
                p,
                down,
                fisher_row,
                numer,
            )
    numer = reduced(tiles)
    asked = request_ids.shape[0] * RANK
    picked, rest = call(
        pick_body,
        [shape((ways, asked, 2 * size), BF), shape((size, rows + 2 * size), BF)],
        numer,
        down,
        prompt_rows,
        q,
        pick_rows,
    )
    parts, own = call(
        join_body,
        [shape((shares, size, rows + 4 * size), BF), shape((asked, 2 * size), BF)],
        swap(picked, "adapter"),
        rest,
    )
    return call(
        serve_body, shape((rows, width), BF), swap(parts, "feature"), own, basis
    )


def solution(mesh):
    placed = (
        P("adapter", None, "feature"),
        P("adapter", None, "feature"),
        P("adapter"),
        P("feature", None),
        P("feature", None),
        P("adapter", "feature"),
        P("adapter"),
    )
    return jax.shard_map(
        on_device, mesh=mesh, in_specs=placed, out_specs=P("adapter", "feature"), check_vma=False
    )
```

time: 602 us -> 346 us (0.57); the launches traced: 592 us -> 345 us
  other arithmetic: 119 us -> 1.17 us
  blocking collectives: 337 us -> 251 us
  Pallas kernels: 0 us -> 49.3 us
  local copies, waits for them, and re-layouts: 34.7 us -> 2.66 us
  matrix products: 29.1 us -> 0 us
  starting transfers between devices: 29.7 us -> 14.5 us
  waiting for transfers between devices: 40.6 us -> 25.8 us
    all_to_all x24 -> x18, blocking collectives: 337 us -> 251 us  [swap(): return lax.all_to_all(parts, axis, 0, 0, tiled=True)]
    another operation x30 -> x0, other arithmetic: 72.4 us -> none  [the longest x18 39.1 us: solve_with(): factor = jnp.linalg.cholesky(gram_sum)]
    pallas_call x0 -> x21, Pallas kernels: none -> 49.3 us  [call(): pl.pallas_call(body, out_shape=outs, in_specs=[whole] * len(args), out_sp...]
    all_to_all x27 -> x0, other arithmetic: 43.6 us -> none  [the longest x21 35.8 us: copy_for_each(): lax.all_to_all(jnp.broadcast_to(shard[None], (count, *shard.shape)), axis...]
    unnamed x66 -> x12, local copies, waits for them, and re-layouts: 27.4 us -> 1.13 us
    dot_general x37 -> x0, matrix products: 24.7 us -> none  [the longest x7 7.09 us: core_of(): return jnp.einsum('irk,irl->ikl', cols_q, rows_p, precision=highest)]
    all_to_all x6 -> x3, starting transfers between devices: 29.7 us -> 14.5 us  [the longest x2 10.6 us: swap(): return lax.all_to_all(parts, axis, 0, 0, tiled=True)]
    all_to_all x6 -> x3, waiting for transfers between devices: 40.6 us -> 25.8 us  [the longest x2 17.9 us: swap(): return lax.all_to_all(parts, axis, 0, 0, tiled=True)]
  transfers between devices with their start and end apart: 6 -> 3, of which waited for: 5 -> 3; matrix products, arithmetic and copies ran while one was open for 4% -> 0% of each run, Pallas kernels for 0% -> 0%
where the time goes in v1:
time: 346 us; the launch traced here: 345 us
  blocking collectives  251 us (73%)
  Pallas kernels  49.3 us (14%)
  waiting for transfers between devices  25.8 us (7%)
  starting transfers between devices  14.5 us (4%)
    all_to_all x18, blocking collectives, swap(): return lax.all_to_all(parts, axis, 0, 0, tiled=True)  251 us
    pallas_call x21, Pallas kernels, call(): pl.pallas_call(body, out_shape=outs, in_specs=[whole] * len(args), out_sp...  49.3 us
    all_to_all x2, waiting for transfers between devices, swap(): return lax.all_to_all(parts, axis, 0, 0, tiled=True)  17.9 us
    all_to_all x2, starting transfers between devices, swap(): return lax.all_to_all(parts, axis, 0, 0, tiled=True)  10.6 us
    all_to_all x1, waiting for transfers between devices, on_device(): lax.all_to_all(jnp.broadcast_to(request_ids[None], (ways, *request_ids.sh...  7.89 us
  transfers between devices with their start and end apart: 3, of which 3 were waited for; matrix products, arithmetic and copies ran while one was open for 0% of the time, Pallas kernels for 0%

profile of v1, /device:TPU:1, one launch (start us, length us, event | category | flops | bytes accessed | tf_op | source)
XLA Modules:
  0.0 344.9 jit_solution(7966591278937267305)
XLA Ops:
  0.0 1.1 convert_bitcast_fusion
  1.1 0.1 copy-done
  1.2 1.0 copy-done.1
  2.2 1.3 shard_map.73
  3.5 6.8 %all-to-all-start = ((bf16[8,64,512]{2,1,0:T(8,128)(2,1)}), bf16[8,64,512]{2,1,0:T(8,128)(2,1)S(1)}, u32[]{:S(2)}, u32[]{:S(2)}) async-start(bf16[8,64,512]{2,1,0:T(8,128)(2,1)} %shard_map.73), calls=%async_computation | async-start | bytes 1048576 | tf_op jit(solution)/shard_map/all_to_all | solution.py:204
  10.3 0.1 broadcast_in_dim_reshape.6.fisher_row
  10.4 9.3 %all-to-all-done.parts = bf16[8,64,512]{2,1,0:T(8,128)(2,1)S(1)} async-done(((bf16[8,64,512]{2,1,0:T(8,128)(2,1)}), bf16[8,64,512]{2,1,0:T(8,128)(2,1)S(1)}, u32[]{:S(2)}, u32[]{:S(2)}) %all-to-all-start) | async-done | bytes 524320 | tf_op jit(solution)/shard_map/all_to_all | solution.py:204
  19.8 1.2 shard_map.74
  21.0 19.5 %all_to_all.106.parts = bf16[32,16,128]{2,1,0:T(8,128)(2,1)S(1)} all-to-all(bf16[32,16,128]{2,1,0:T(8,128)(2,1)S(1)} %get-tuple-element.22), channel_id=1, replica_groups=mesh['adapter'=32,'feature'=8] {'adapter'}, dimensions={0} | all-to-all | bytes 262144 | tf_op jit(solution)/shard_map/all_to_all | solution.py:204
  40.5 12.7 %all_to_all.107.tiles = bf16[32,16,128]{2,1,0:T(8,128)(2,1)S(1)} all-to-all(bf16[32,16,128]{2,1,0:T(8,128)(2,1)S(1)} %shard_map.75), channel_id=1, replica_groups=mesh['adapter'=32,'feature'=8] {'adapter'}, dimensions={0} | all-to-all | bytes 262144 | tf_op jit(solution)/shard_map/all_to_all | solution.py:204
  53.2 0.4 shard_map.76
  53.6 14.1 %all_to_all.108.parts = bf16[8,64,384]{2,1,0:T(8,128)(2,1)S(1)} all-to-all(bf16[8,64,384]{2,1,0:T(8,128)(2,1)S(1)} %shard_map.76), channel_id=1, replica_groups=mesh['adapter'=32,'feature'=8] {'feature'}, dimensions={0} | all-to-all | bytes 786432 | tf_op jit(solution)/shard_map/all_to_all | solution.py:204
  67.6 6.8 %shard_map.77 = (bf16[32,16,128]{2,1,0:T(8,128)(2,1)S(1)}, f32[64,256]{1,0:T(8,128)S(1)}) custom-call(bf16[8,64,384]{2,1,0:T(8,128)(2,1)S(1)} %all_to_all.108.parts, f32[64,256]{1,0:T(8,128)S(1)} %get-tuple-element.23.other, bf16[256,1024]{1,0:T(8,128)(2,1)S(1)} %bitcast.14, f32[1,256]{1,0:T(1,128)S(1)} %broadcast_in_dim_reshape.6.fisher_row), custom_call_target="tpu_custom_call" | custom-call | tf_op jit(solution)/shard_map/pallas_call | solution.py:18
  74.4 12.3 %all_to_all.109.parts = bf16[32,16,128]{2,1,0:T(8,128)(2,1)S(1)} all-to-all(bf16[32,16,128]{2,1,0:T(8,128)(2,1)S(1)} %get-tuple-element.24), channel_id=1, replica_groups=mesh['adapter'=32,'feature'=8] {'adapter'}, dimensions={0} | all-to-all | bytes 262144 | tf_op jit(solution)/shard_map/all_to_all | solution.py:204
  86.8 12.7 %all_to_all.110.tiles = bf16[32,16,128]{2,1,0:T(8,128)(2,1)S(1)} all-to-all(bf16[32,16,128]{2,1,0:T(8,128)(2,1)S(1)} %shard_map.78), channel_id=1, replica_groups=mesh['adapter'=32,'feature'=8] {'adapter'}, dimensions={0} | all-to-all | bytes 262144 | tf_op jit(solution)/shard_map/all_to_all | solution.py:204
  99.5 0.4 shard_map.79
  99.9 13.8 %all_to_all.111.parts = bf16[8,64,384]{2,1,0:T(8,128)(2,1)S(1)} all-to-all(bf16[8,64,384]{2,1,0:T(8,128)(2,1)S(1)} %shard_map.79), channel_id=1, replica_groups=mesh['adapter'=32,'feature'=8] {'feature'}, dimensions={0} | all-to-all | bytes 786432 | tf_op jit(solution)/shard_map/all_to_all | solution.py:204
  113.7 6.8 %shard_map.80 = (bf16[32,16,128]{2,1,0:T(8,128)(2,1)S(1)}, f32[64,256]{1,0:T(8,128)S(1)}) custom-call(bf16[8,64,384]{2,1,0:T(8,128)(2,1)S(1)} %all_to_all.111.parts, f32[64,256]{1,0:T(8,128)S(1)} %get-tuple-element.25.other, bf16[256,1024]{1,0:T(8,128)(2,1)S(1)} %bitcast.9, f32[1,256]{1,0:T(1,128)S(1)} %broadcast_in_dim_reshape.6.fisher_row), custom_call_target="tpu_custom_call" | custom-call | tf_op jit(solution)/shard_map/pallas_call | solution.py:18
  120.5 12.3 %all_to_all.112.parts = bf16[32,16,128]{2,1,0:T(8,128)(2,1)S(1)} all-to-all(bf16[32,16,128]{2,1,0:T(8,128)(2,1)S(1)} %get-tuple-element.26), channel_id=1, replica_groups=mesh['adapter'=32,'feature'=8] {'adapter'}, dimensions={0} | all-to-all | bytes 262144 | tf_op jit(solution)/shard_map/all_to_all | solution.py:204
  132.9 12.7 %all_to_all.113.tiles = bf16[32,16,128]{2,1,0:T(8,128)(2,1)S(1)} all-to-all(bf16[32,16,128]{2,1,0:T(8,128)(2,1)S(1)} %shard_map.81), channel_id=1, replica_groups=mesh['adapter'=32,'feature'=8] {'adapter'}, dimensions={0} | all-to-all | bytes 262144 | tf_op jit(solution)/shard_map/all_to_all | solution.py:204
  145.6 0.4 shard_map.82
  146.0 13.8 %all_to_all.114.parts = bf16[8,64,384]{2,1,0:T(8,128)(2,1)S(1)} all-to-all(bf16[8,64,384]{2,1,0:T(8,128)(2,1)S(1)} %shard_map.82), channel_id=1, replica_groups=mesh['adapter'=32,'feature'=8] {'feature'}, dimensions={0} | all-to-all | bytes 786432 | tf_op jit(solution)/shard_map/all_to_all | solution.py:204
  159.8 6.8 %shard_map.83 = (bf16[32,16,128]{2,1,0:T(8,128)(2,1)S(1)}, f32[64,256]{1,0:T(8,128)S(1)}) custom-call(bf16[8,64,384]{2,1,0:T(8,128)(2,1)S(1)} %all_to_all.114.parts, f32[64,256]{1,0:T(8,128)S(1)} %get-tuple-element.27.other, bf16[256,1024]{1,0:T(8,128)(2,1)S(1)} %bitcast.16, f32[1,256]{1,0:T(1,128)S(1)} %broadcast_in_dim_reshape.6.fisher_row), custom_call_target="tpu_custom_call" | custom-call | tf_op jit(solution)/shard_map/pallas_call | solution.py:18
  166.6 12.3 %all_to_all.115.parts = bf16[32,16,128]{2,1,0:T(8,128)(2,1)S(1)} all-to-all(bf16[32,16,128]{2,1,0:T(8,128)(2,1)S(1)} %get-tuple-element.28), channel_id=1, replica_groups=mesh['adapter'=32,'feature'=8] {'adapter'}, dimensions={0} | all-to-all | bytes 262144 | tf_op jit(solution)/shard_map/all_to_all | solution.py:204
  179.0 12.7 %all_to_all.116.tiles = bf16[32,16,128]{2,1,0:T(8,128)(2,1)S(1)} all-to-all(bf16[32,16,128]{2,1,0:T(8,128)(2,1)S(1)} %shard_map.84), channel_id=1, replica_groups=mesh['adapter'=32,'feature'=8] {'adapter'}, dimensions={0} | all-to-all | bytes 262144 | tf_op jit(solution)/shard_map/all_to_all | solution.py:204
  191.7 0.4 shard_map.85
  192.1 13.8 %all_to_all.117.parts = bf16[8,64,384]{2,1,0:T(8,128)(2,1)S(1)} all-to-all(bf16[8,64,384]{2,1,0:T(8,128)(2,1)S(1)} %shard_map.85), channel_id=1, replica_groups=mesh['adapter'=32,'feature'=8] {'feature'}, dimensions={0} | all-to-all | bytes 786432 | tf_op jit(solution)/shard_map/all_to_all | solution.py:204
  205.9 6.8 %shard_map.86 = (bf16[32,16,128]{2,1,0:T(8,128)(2,1)S(1)}, f32[64,256]{1,0:T(8,128)S(1)}) custom-call(bf16[8,64,384]{2,1,0:T(8,128)(2,1)S(1)} %all_to_all.117.parts, f32[64,256]{1,0:T(8,128)S(1)} %get-tuple-element.29.other, bf16[256,1024]{1,0:T(8,128)(2,1)S(1)} %bitcast.11, f32[1,256]{1,0:T(1,128)S(1)} %broadcast_in_dim_reshape.6.fisher_row), custom_call_target="tpu_custom_call" | custom-call | tf_op jit(solution)/shard_map/pallas_call | solution.py:18
  212.7 12.3 %all_to_all.118.parts = bf16[32,16,128]{2,1,0:T(8,128)(2,1)S(1)} all-to-all(bf16[32,16,128]{2,1,0:T(8,128)(2,1)S(1)} %get-tuple-element.30), channel_id=1, replica_groups=mesh['adapter'=32,'feature'=8] {'adapter'}, dimensions={0} | all-to-all | bytes 262144 | tf_op jit(solution)/shard_map/all_to_all | solution.py:204
  225.1 12.7 %all_to_all.119.tiles.numer_tiles = bf16[32,16,128]{2,1,0:T(8,128)(2,1)S(1)} all-to-all(bf16[32,16,128]{2,1,0:T(8,128)(2,1)S(1)} %shard_map.87), channel_id=1, replica_groups=mesh['adapter'=32,'feature'=8] {'adapter'}, dimensions={0} | all-to-all | bytes 262144 | tf_op jit(solution)/shard_map/all_to_all | solution.py:204
  237.8 0.4 shard_map.88
  238.2 13.8 %all_to_all.120.parts = bf16[8,64,384]{2,1,0:T(8,128)(2,1)S(1)} all-to-all(bf16[8,64,384]{2,1,0:T(8,128)(2,1)S(1)} %shard_map.88), channel_id=1, replica_groups=mesh['adapter'=32,'feature'=8] {'feature'}, dimensions={0} | all-to-all | bytes 786432 | tf_op jit(solution)/shard_map/all_to_all | solution.py:204
  252.0 7.0 %shard_map.89 = (bf16[32,16,128]{2,1,0:T(8,128)(2,1)S(1)}, f32[64,256]{1,0:T(8,128)S(1)}, bf16[64,1024]{1,0:T(8,128)(2,1)S(1)}) custom-call(bf16[8,64,384]{2,1,0:T(8,128)(2,1)S(1)} %all_to_all.120.parts, f32[64,256]{1,0:T(8,128)S(1)} %get-tuple-element.31.other, bf16[256,1024]{1,0:T(8,128)(2,1)S(1)} %bitcast.18, ...), custom_call_target="tpu_custom_call" | custom-call | tf_op jit(solution)/shard_map/pallas_call | solution.py:18
  259.1 12.5 %all_to_all.121.parts = bf16[32,16,128]{2,1,0:T(8,128)(2,1)S(1)} all-to-all(bf16[32,16,128]{2,1,0:T(8,128)(2,1)S(1)} %get-tuple-element.32), channel_id=1, replica_groups=mesh['adapter'=32,'feature'=8] {'adapter'}, dimensions={0} | all-to-all | bytes 262144 | tf_op jit(solution)/shard_map/all_to_all | solution.py:204
  271.5 0.6 broadcast_in_dim.13
  272.1 3.8 %all-to-all-start.18 = ((s32[32,1,4]{2,1,0:T(1,128)}), s32[32,1,4]{2,1,0:T(1,128)S(1)}, u32[]{:S(2)}, u32[]{:S(2)}) async-start(s32[32,1,4]{2,1,0:T(1,128)} %broadcast_in_dim.13), calls=%async_computation.18 | async-start | bytes 32768 | tf_op jit(solution)/shard_map/all_to_all | solution.py:220
  276.0 0.7 shard_map.90
  276.7 7.9 %all-to-all-done.18 = s32[32,1,4]{2,1,0:T(1,128)S(1)} async-done(((s32[32,1,4]{2,1,0:T(1,128)}), s32[32,1,4]{2,1,0:T(1,128)S(1)}, u32[]{:S(2)}, u32[]{:S(2)}) %all-to-all-start.18) | async-done | bytes 544 | tf_op jit(solution)/shard_map/all_to_all | solution.py:220
  284.6 3.9 %all-to-all-start.17 = ((bf16[32,16,128]{2,1,0:T(8,128)(2,1)}), bf16[32,16,128]{2,1,0:T(8,128)(2,1)S(1)}, u32[]{:S(2)}, u32[]{:S(2)}) async-start(bf16[32,16,128]{2,1,0:T(8,128)(2,1)} %shard_map.90), calls=%async_computation.17 | async-start | bytes 262144 | tf_op jit(solution)/shard_map/all_to_all | solution.py:204
  288.5 0.1 sub.11
  288.6 0.1 broadcast_in_dim.14
  288.7 0.6 broadcast_in_dim_reshape.8.ids
  289.3 8.6 %all-to-all-done.17.tiles = bf16[32,16,128]{2,1,0:T(8,128)(2,1)S(1)} async-done(((bf16[32,16,128]{2,1,0:T(8,128)(2,1)}), bf16[32,16,128]{2,1,0:T(8,128)(2,1)S(1)}, u32[]{:S(2)}, u32[]{:S(2)}) %all-to-all-start.17) | async-done | bytes 131104 | tf_op jit(solution)/shard_map/all_to_all | solution.py:204
  297.9 1.2 shard_map.91
  299.0 16.0 %all_to_all.122.parts = bf16[32,64,128]{2,1,0:T(8,128)(2,1)S(1)} all-to-all(bf16[32,64,128]{2,1,0:T(8,128)(2,1)S(1)} %get-tuple-element.34), channel_id=1, replica_groups=mesh['adapter'=32,'feature'=8] {'adapter'}, dimensions={0} | all-to-all | bytes 1048576 | tf_op jit(solution)/shard_map/all_to_all | solution.py:204
  315.0 0.1 shard_map.92
  315.1 21.1 %all_to_all.123.parts = bf16[8,64,768]{2,1,0:T(8,128)(2,1)S(1)} all-to-all(bf16[8,64,768]{2,1,0:T(8,128)(2,1)S(1)} %get-tuple-element.36), channel_id=1, replica_groups=mesh['adapter'=32,'feature'=8] {'feature'}, dimensions={0} | all-to-all | bytes 1572864 | tf_op jit(solution)/shard_map/all_to_all | solution.py:204
  336.3 8.7 %shard_map.93 = bf16[512,1024]{1,0:T(8,128)(2,1)} custom-call(bf16[8,64,768]{2,1,0:T(8,128)(2,1)S(1)} %all_to_all.123.parts, bf16[64,128]{1,0:T(8,128)(2,1)S(1)} %get-tuple-element.37.own, bf16[64,1024]{1,0:T(8,128)(2,1)S(1)} %get-tuple-element.38.basis), custom_call_target="tpu_custom_call" | custom-call | tf_op jit(solution)/shard_map/pallas_call | solution.py:18
  (17 shorter events, 0.4 us)
Async XLA Ops:
  0.0 1.2 copy-start
  1.2 1.0 copy-start.1
  3.5 6.8 %copy-start.4 = (f32[16]{0:T(128)S(1)}, f32[16]{0:T(128)}, u32[]{:S(2)}) copy-start(f32[16]{0:T(128)} %param.9) | copy-start | bytes 196
  3.5 16.3 %all-to-all-start = ((bf16[8,64,512]{2,1,0:T(8,128)(2,1)}), bf16[8,64,512]{2,1,0:T(8,128)(2,1)S(1)}, u32[]{:S(2)}, u32[]{:S(2)}) async-start(bf16[8,64,512]{2,1,0:T(8,128)(2,1)} %shard_map.73), calls=%async_computation | async-start | bytes 1048576 | tf_op jit(solution)/shard_map/all_to_all | solution.py:204
  53.6 14.1 %copy-start.2 = (bf16[16,16,1024]{2,1,0:T(8,128)(2,1)S(1)}, bf16[16,16,1024]{2,1,0:T(8,128)(2,1)}, u32[]{:S(2)}) copy-start(bf16[16,16,1024]{2,1,0:T(8,128)(2,1)} %param.7) | copy-start | bytes 1572868
  252.0 19.5 %copy-start.5 = (s32[4]{0:T(128)S(1)}, s32[4]{0:T(128)}, u32[]{:S(2)}) copy-start(s32[4]{0:T(128)} %param.13) | copy-start | bytes 52
  259.0 38.8 %copy-start.3 = (bf16[512,1024]{1,0:T(8,128)(2,1)S(1)}, bf16[512,1024]{1,0:T(8,128)(2,1)}, u32[]{:S(2)}) copy-start(bf16[512,1024]{1,0:T(8,128)(2,1)} %prompts.1) | copy-start | bytes 3145732
  272.1 12.4 %all-to-all-start.18 = ((s32[32,1,4]{2,1,0:T(1,128)}), s32[32,1,4]{2,1,0:T(1,128)S(1)}, u32[]{:S(2)}, u32[]{:S(2)}) async-start(s32[32,1,4]{2,1,0:T(1,128)} %broadcast_in_dim.13), calls=%async_computation.18 | async-start | bytes 32768 | tf_op jit(solution)/shard_map/all_to_all | solution.py:220
  284.6 13.3 %all-to-all-start.17 = ((bf16[32,16,128]{2,1,0:T(8,128)(2,1)}), bf16[32,16,128]{2,1,0:T(8,128)(2,1)S(1)}, u32[]{:S(2)}, u32[]{:S(2)}) async-start(bf16[32,16,128]{2,1,0:T(8,128)(2,1)} %shard_map.90), calls=%async_computation.17 | async-start | bytes 262144 | tf_op jit(solution)/shard_map/all_to_all | solution.py:204
